TPU v7x, 256 devices: a whole 4x4x8 slice. The times are simulated.
256 devices in a mesh: row: 8 (over z_hi, x), col: 32 (over y, z_lo, core).
Axes of the slice: x: 4, y: 4, z: 8 (z_hi: 2, z_lo: 4; z = z_hi * 4 + z_lo), core: 2. Of those that a mesh axis runs over, the one named last changes fastest.
Arguments:
- inputs: bfloat16 [512, 12288], P('col', 'row'), may hold values from -6 to 6
- up_weight: bfloat16 [12288, 24576], P('row', 'col'), may hold values from -0.0546875 to 0.0546875
- down_weight: bfloat16 [24576, 12288], P('col', 'row'), may hold values from -0.0390625 to 0.0390625
- out_grad: bfloat16 [512, 12288], P('col', 'row'), may hold values from -6 to 6
Outputs:
- outputs: bfloat16 [512, 12288], P('col', 'row')
- in_grad: bfloat16 [512, 12288], P('col', 'row')
- up_grad: bfloat16 [12288, 24576], P('row', 'col')
- down_grad: bfloat16 [24576, 12288], P('col', 'row')
All inputs are finite; a program needn't handle non-finite values.
Results may differ from a plain program's by a relative error of at most 0.005.
Values may be sent and summed in bfloat16 or wider, within the bound.
A program may use at most 64 MiB of HBM per device.

v0:
```python
import jax
import jax.numpy as jnp
from jax import lax
from jax.sharding import PartitionSpec as P

gelu_coef = 0.7978845608
cube_coef = 0.044715


def activate(hidden):
    tangent = jnp.tanh(gelu_coef * (hidden + cube_coef * hidden * hidden * hidden))
    return 0.5 * hidden * (1.0 + tangent)


def slope(hidden):
    tangent = jnp.tanh(gelu_coef * (hidden + cube_coef * hidden * hidden * hidden))
    inner = gelu_coef * (1.0 + 3.0 * cube_coef * hidden * hidden)
    return 0.5 * (1.0 + tangent) + 0.5 * hidden * (1.0 - tangent * tangent) * inner


def shards(inputs, up_weight, down_weight, out_grad):
    first = (((0,), (0,)), ((), ()))
    second = (((1,), (1,)), ((), ()))
    token_rows = lax.all_gather(inputs, "col", axis=0, tiled=True)
    hidden = lax.psum(jnp.dot(token_rows, up_weight, preferred_element_type=jnp.float32), "row")
    active = activate(hidden).astype(jnp.bfloat16)
    block = active
    outputs = lax.psum_scatter(
        jnp.dot(block, down_weight, preferred_element_type=jnp.float32),
        "col",
        scatter_dimension=0,
        tiled=True,
    ).astype(jnp.bfloat16)
    upstream = lax.all_gather(out_grad, "col", axis=0, tiled=True)
    down_grad = lax.dot_general(active, upstream, first, preferred_element_type=jnp.float32).astype(
        jnp.bfloat16
    )
    act_grad = lax.psum(
        lax.dot_general(upstream, down_weight, second, preferred_element_type=jnp.float32), "row"
    )
    hid_grad = (act_grad * slope(hidden)).astype(jnp.bfloat16)
    up_grad = lax.dot_general(
        token_rows, hid_grad, first, preferred_element_type=jnp.float32
    ).astype(jnp.bfloat16)
    block = hid_grad
    in_grad = lax.psum_scatter(
        lax.dot_general(block, up_weight, second, preferred_element_type=jnp.float32),
        "col",
        scatter_dimension=0,
        tiled=True,
    ).astype(jnp.bfloat16)
    return (outputs, in_grad, up_grad, down_grad)


def solution(mesh):
    in_specs = (P("col", "row"), P("row", "col"), P("col", "row"), P("col", "row"))
    out_specs = (P("col", "row"), P("col", "row"), P("row", "col"), P("col", "row"))
    return jax.shard_map(shards, mesh=mesh, in_specs=in_specs, out_specs=out_specs, check_vma=False)
```

profile of v0, /device:TPU:1, one launch (start us, length us, event | category | flops | bytes accessed | tf_op | source)
XLA Modules:
  0.0 607.9 jit_solution(11108096432556507894)
XLA Ops:
  7.2 0.0 copy-start
  7.2 0.0 all-gather.3.cloned.1.call-start
  7.2 0.7 all-gather.3.cloned.1.call-update
  7.9 0.0 all-gather.5.cloned.1.call-start
  8.0 0.7 all-gather.5.cloned.1.call-update
  8.7 0.0 all-reduce.3.cloned.1.call-start
  8.7 65.1 %all-gather.3.cloned.1.call-done = bf16[512,1536]{1,0:T(8,128)(2,1)} async-done(((bf16[16,1536]{1,0:T(8,128)(2,1)}), bf16[512,1536]{1,0:T(8,128)(2,1)}) %all-gather.3.cloned.1.call-update) | async-done | bytes 1572880 | tf_op jit(solution)/shard_map/all_gather | solution.py:24
  73.8 0.0 copy-done
  73.8 3.9 fusion.10
  77.7 56.6 %all-gather.5.cloned.1.call-done = bf16[512,1536]{1,0:T(8,128)(2,1)} async-done(((bf16[16,1536]{1,0:T(8,128)(2,1)}), bf16[512,1536]{1,0:T(8,128)(2,1)}) %all-gather.5.cloned.1.call-update) | async-done | bytes 1572880 | tf_op jit(solution)/shard_map/all_gather | solution.py:34
  134.3 4.7 fusion.11
  139.0 0.0 all-reduce.3.cloned.1.call-update
  139.0 0.0 reduce-scatter.5.cloned.1.call-start
  139.1 160.4 %all-reduce.3.cloned.1.call-done = (f32[512,768]{1,0:T(8,128)}, f32[512,768]{1,0:T(8,128)}) async-done(((f32[512,768]{1,0:T(8,128)}, f32[512,768]{1,0:T(8,128)}), (f32[512,768]{1,0:T(8,128)}, f32[512,768]{1,0:T(8,128)})) %all-reduce.3.cloned.1.call-update) | async-done | bytes 3145744 | tf_op jit(solution)/shard_map/psum | solution.py:25
  299.4 2.9 fusion.8
  302.3 3.1 fusion.12
  305.4 0.0 reduce-scatter.5.cloned.1.call-update
  305.4 0.0 reduce-scatter.3.cloned.1.call-start
  305.5 5.2 fusion.9
  310.7 0.0 reduce-scatter.3.cloned.1.call-update
  310.8 4.2 fusion
  315.0 4.3 copy.8
  319.3 4.8 convolution_convert_fusion
  324.1 127.0 %reduce-scatter.5.cloned.1.call-done = f32[16,1536]{1,0:T(8,128)} async-done(((f32[512,1536]{1,0:T(8,128)}), f32[16,1536]{1,0:T(8,128)}) %reduce-scatter.5.cloned.1.call-update) | async-done | bytes 98320 | tf_op jit(solution)/shard_map/reduce_scatter | solution.py:46
  451.1 1.5 convert_element_type.24
  452.6 147.2 %reduce-scatter.3.cloned.1.call-done = f32[16,1536]{1,0:T(8,128)} async-done(((f32[512,1536]{1,0:T(8,128)}), f32[16,1536]{1,0:T(8,128)}) %reduce-scatter.3.cloned.1.call-update) | async-done | bytes 98320 | tf_op jit(solution)/shard_map/reduce_scatter | solution.py:28
  599.9 1.5 convert_element_type.22
Async XLA Ops:
  7.2 66.6 %copy-start = (bf16[1536,768]{1,0:T(8,128)(2,1)S(1)}, bf16[1536,768]{1,0:T(8,128)(2,1)}, u32[]{:S(2)}) copy-start(bf16[1536,768]{1,0:T(8,128)(2,1)} %param.5) | copy-start | bytes 7077892
  7.2 66.6 %all-gather.3.cloned.1.call-start = ((), (), s32[]{:S(2)}) async-start(), calls=%async_computation.2 | async-start | bytes 1622016 | tf_op jit(solution)/shard_map/all_gather | solution.py:24
  7.9 126.4 %all-gather.5.cloned.1.call-start = ((), (), s32[]{:S(2)}) async-start(), calls=%async_computation.4 | async-start | bytes 1622016 | tf_op jit(solution)/shard_map/all_gather | solution.py:34
  8.7 290.8 %all-reduce.3.cloned.1.call-start = ((), (), s32[]{:S(2)}) async-start(), calls=%async_computation.6 | async-start | bytes 6291456 | tf_op jit(solution)/shard_map/psum | solution.py:25
  139.0 312.1 %reduce-scatter.5.cloned.1.call-start = ((), (), s32[]{:S(2)}) async-start(), calls=%async_computation.5 | async-start | bytes 3244032 | tf_op jit(solution)/shard_map/reduce_scatter | solution.py:46
  305.4 294.4 %reduce-scatter.3.cloned.1.call-start = ((), (), s32[]{:S(2)}) async-start(), calls=%async_computation.3 | async-start | bytes 3244032 | tf_op jit(solution)/shard_map/reduce_scatter | solution.py:28
Sparse Core Ops, SparseCore 0:
  9.9 63.8 all-gather.2
  75.6 58.6 all-gather.4
  139.1 160.2 all-reduce.2
  305.6 145.5 reduce-scatter.4
  453.7 146.1 reduce-scatter.2
where the time goes:
time: 613 us; the launch traced here: 608 us
  waiting for transfers between devices  558 us (91%)
  matrix products  26 us (4%)
  between operations  13.8 us (2%)
    psum x1, waiting for transfers between devices, shards(): lax.psum(jnp.dot(token_rows, up_weight, preferred_element_type=jnp.float3...  160 us
    reduce_scatter x1, waiting for transfers between devices, shards(): lax.psum_scatter(jnp.dot(block, down_weight, preferred_element_type=jnp.f...  147 us
    reduce_scatter x1, waiting for transfers between devices, shards(): lax.psum_scatter(lax.dot_general(block, up_weight, second, preferred_elem...  127 us
    all_gather x1, waiting for transfers between devices, shards(): token_rows = lax.all_gather(inputs, 'col', axis=0, tiled=True)  65.1 us
    all_gather x1, waiting for transfers between devices, shards(): upstream = lax.all_gather(out_grad, 'col', axis=0, tiled=True)  56.6 us
  transfers between devices with their start and end apart: 5, of which 5 were waited for; matrix products, arithmetic and copies ran while one was open for 4% of the time, Pallas kernels for 0%

commit v1 on v0

v1 whole, which is shorter than its diff:
```python
import functools

import jax
import jax.numpy as jnp
from jax import lax
from jax.experimental import pallas as pl
from jax.experimental.pallas import tpu as pltpu
from jax.sharding import PartitionSpec as P

MESH = pl.DeviceIdType.MESH
F32, BF16 = jnp.float32, jnp.bfloat16

gelu_coef = 0.7978845608
cube_coef = 0.044715

ORDER = (
    ("first", 0, 0), ("first", 1, 0), ("weights", 0, 0),
    ("relay", 0, 1), ("relay", 0, 2), ("relay", 0, 3),
    ("up", 0, 0),
    ("relay", 1, 1), ("relay", 1, 2),
    ("pass", 0, 1), ("relay", 1, 3), ("pass", 0, 3), ("pass", 0, 2),
    ("up", 0, 1), ("rowsum", 0, 0), ("up", 1, 0), ("up", 0, 3), ("up", 0, 2),
    ("act", 0, 0), ("rowsum", 0, 1),
    ("pass", 1, 1), ("pass", 1, 3), ("pass", 1, 2),
    ("up", 1, 1), ("spread", 0, 0), ("rowsum", 1, 0), ("up", 1, 3), ("act", 0, 1), ("up", 1, 2),
    ("rowsum", 0, 3), ("act", 1, 0), ("rowsum", 0, 2), ("spread", 0, 1),
    ("act", 0, 3), ("rowsum", 1, 1), ("spread", 1, 0), ("act", 0, 2),
    ("down", 0, 0), ("spread", 0, 3), ("act", 1, 1), ("rowsum", 1, 3), ("spread", 0, 2),
    ("pair", 0, 0), ("rowsum", 1, 2), ("spread", 1, 1), ("act", 1, 3),
    ("down", 0, 1), ("act", 1, 2), ("down", 1, 0), ("spread", 1, 3), ("pair", 0, 1),
    ("spread", 1, 2), ("down", 0, 3), ("pair", 1, 0), ("down", 0, 2), ("pair", 0, 3),
    ("pair", 0, 2), ("down", 1, 1), ("down", 1, 3), ("pair", 1, 1), ("down", 1, 2), ("pair", 1, 3),
    ("colsum", 0, 0), ("pair", 1, 2), ("grad", 0, 0), ("colsum", 1, 0), ("grad", 1, 0),
    ("finish", 0, 0), ("finish", 1, 0),
)


def kernel(
    x_ref, g_ref, wu_hbm, wd_hbm,
    out_ref, in_grad_ref, up_grad_hbm, down_grad_hbm,
    wu, wd, wut, wdt, gather, part, send_x, recv_x, own_x, send_z, recv_z, slopes, act,
    prod, recv_c, send_y, recv_y, own_y, send_f, recv_f, own_f, up_grad, down_grad,
    wsem, osem, sent, gz, gy, gs, gs0, rx, rz, az, ax, rc, ry, rf,
):
    row, col = lax.axis_index("row"), lax.axis_index("col")
    x, h = lax.rem(row, 4), row // 4
    y, zl, k = col // 8, lax.rem(col // 2, 4), lax.rem(col, 2)

    def at(dx=0, dh=0, dy=0, dz=0, dk=0):
        r = lax.rem(h + dh, 2) * 4 + lax.rem(x + dx, 4)
        c = lax.rem(y + dy, 4) * 8 + lax.rem(zl + dz, 4) * 2 + lax.rem(k + dk, 2)
        return (r, c)

    loads = [
        pltpu.make_async_copy(wu_hbm, wu, wsem.at[0]),
        pltpu.make_async_copy(wd_hbm, wd, wsem.at[1]),
    ]
    for load in loads:
        load.start()

    barrier = pltpu.get_barrier_semaphore()
    partners = [dict(dk=1), dict(dh=1)]
    for j in (1, 2, 3):
        partners += [dict(dx=j), dict(dy=j), dict(dz=j)]
    for partner in partners:
        pl.semaphore_signal(barrier, inc=1, device_id=at(**partner), device_id_type=MESH)
    pl.semaphore_wait(barrier, len(partners))

    sends = []

    def send(src, dst, sem, **where):
        copy = pltpu.make_async_remote_copy(
            src_ref=src, dst_ref=dst, send_sem=sent.at[len(sends)], recv_sem=sem,
            device_id=at(**where), device_id_type=MESH,
        )
        copy.start()
        sends.append(copy)

    def arrive(dst, sem):
        pltpu.make_async_remote_copy(
            src_ref=dst, dst_ref=dst, send_sem=sent.at[0], recv_sem=sem,
            device_id=at(dk=1), device_id_type=MESH,
        ).wait_recv()

    def rows(start, size):
        return pl.ds(pl.multiple_of(start, 16), size)

    def place(core, z):
        return rows(core * 64 + z * 16, 16)

    sources = (x_ref, g_ref)

    def first(c, _):
        src = sources[c]
        for j in (1, 2, 3):
            send(src, gather.at[c, 0, place(k, zl)], gz.at[c, j - 1], dz=j)
        for d in (1, 3, 2):
            send(src, gather.at[c, 4 - d, place(k, zl)], gy.at[c, 4 - d, 0], dy=d)
        send(src, gather.at[c, 0, place(k, zl)], gs0.at[c, 0], dk=1)
        gather[c, 0, place(k, zl)] = src[...]

    def weights(c, _):
        for load in loads:
            load.wait()
        for j in range(3):
            wut[j * 256:(j + 1) * 256, :] = wu[:, j * 256:(j + 1) * 256].T
        for j in range(6):
            wdt[j * 256:(j + 1) * 256, :] = wd[:, j * 256:(j + 1) * 256].T

    def relay(c, j):
        piece = gather.at[c, 0, place(k, lax.rem(zl + 4 - j, 4))]
        arrive(piece, gz.at[c, j - 1])
        for d in (1, 3, 2):
            send(piece, gather.at[c, 4 - d, place(k, lax.rem(zl + 4 - j, 4))], gy.at[c, 4 - d, j], dy=d)
        send(piece, piece, gs0.at[c, j], dk=1)

    def pass_on(c, d):
        for j in range(4):
            arrive(gather.at[c, d, place(k, lax.rem(zl + 4 - j, 4))], gy.at[c, d, j])
        half = gather.at[c, d, rows(k * 64, 64)]
        send(half, half, gs.at[c, d], dk=1)

    def up(c, d):
        if d == 0:
            for j in range(4):
                arrive(gather.at[c, 0, place(1 - k, lax.rem(zl + 4 - j, 4))], gs0.at[c, j])
        else:
            arrive(gather.at[c, d, rows((1 - k) * 64, 64)], gs.at[c, d])
        weight = (wu, wdt)[c]
        part[c, d] = jnp.dot(gather[c, d], weight[...], preferred_element_type=F32)
        send_x[c, d] = part[c, d].astype(BF16)
        for j in (1, 3, 2):
            send(send_x.at[c, d, rows(lax.rem(x + j, 4) * 32, 32)], recv_x.at[c, d, j - 1], rx.at[c, d, j - 1], dx=j)

    def rowsum(c, d):
        for j in (1, 2, 3):
            arrive(recv_x.at[c, d, j - 1], rx.at[c, d, j - 1])
        total = part[c, d, rows(x * 32, 32)]
        for j in (1, 2, 3):
            total = total + recv_x[c, d, j - 1].astype(F32)
        own_x[c, d] = total
        send_z[c, d] = own_x[c, d, rows((1 - h) * 16, 16)].astype(BF16)
        send(send_z.at[c, d], recv_z.at[c, d], rz.at[c, d], dh=1)

    def mine(half):
        return rows(x * 32 + half * 16, 16)

    def act_step(c, d):
        arrive(recv_z.at[c, d], rz.at[c, d])
        total = own_x[c, d, rows(h * 16, 16)] + recv_z[c, d].astype(F32)
        if c == 0:
            tangent = jnp.tanh(gelu_coef * (total + cube_coef * total * total * total))
            inner = gelu_coef * (1.0 + 3.0 * cube_coef * total * total)
            slopes[d] = 0.5 * (1.0 + tangent) + 0.5 * total * (1.0 - tangent * tangent) * inner
            result = 0.5 * total * (1.0 + tangent)
        else:
            result = total * slopes[d]
        act[c, d, mine(h)] = result.astype(BF16)
        send(act.at[c, d, mine(h)], act.at[c, d, mine(h)], az.at[c, d], dh=1)

    def spread(c, d):
        arrive(act.at[c, d, mine(1 - h)], az.at[c, d])
        for j in (1, 3, 2):
            send(act.at[c, d, rows(x * 32, 32)], act.at[c, d, rows(x * 32, 32)], ax.at[c, d, j - 1], dx=j)

    def down(c, d):
        for j in (1, 2, 3):
            arrive(act.at[c, d, rows(lax.rem(x + 4 - j, 4) * 32, 32)], ax.at[c, d, j - 1])
        weight = (wd, wut)[c]
        prod[c, d] = jnp.dot(act[c, d], weight[...], preferred_element_type=F32)
        send(prod.at[c, d, rows((1 - k) * 64, 64)], recv_c.at[c, d], rc.at[c, d], dk=1)

    def pair(c, d):
        arrive(recv_c.at[c, d], rc.at[c, d])
        total = prod[c, d, rows(k * 64, 64)] + recv_c[c, d]
        if d == 0:
            own_y[c] = total
        else:
            send_y[c, d - 1] = total.astype(BF16)
            send(send_y.at[c, d - 1], recv_y.at[c, d - 1], ry.at[c, d - 1], dy=d)

    def colsum(c, _):
        for d in (1, 2, 3):
            arrive(recv_y.at[c, d - 1], ry.at[c, d - 1])
        total = own_y[c]
        for d in (1, 2, 3):
            total = total + recv_y[c, d - 1].astype(F32)
        own_y[c] = total
        send_f[c] = total.astype(BF16)
        for j in (1, 3, 2):
            send(send_f.at[c, rows(lax.rem(zl + j, 4) * 16, 16)], recv_f.at[c, j - 1], rf.at[c, j - 1], dz=j)

    results = (out_ref, in_grad_ref)

    def finish(c, _):
        for j in (1, 2, 3):
            arrive(recv_f.at[c, j - 1], rf.at[c, j - 1])
        total = own_y[c, rows(zl * 16, 16)]
        for j in (1, 2, 3):
            total = total + recv_f[c, j - 1].astype(F32)
        results[c][...] = total.astype(BF16)

    stores = []

    def grad(c, _):
        left, right = ((act, gather), (gather, act))[c]
        target, home = ((down_grad, down_grad_hbm), (up_grad, up_grad_hbm))[c]
        a = left[0, :].reshape(512, left.shape[3])
        width = right.shape[3]
        for n in range(0, width, 256):
            b = right[1, :, :, n:n + 256].reshape(512, 256)
            target[:, n:n + 256] = lax.dot_general(
                a, b, (((0,), (0,)), ((), ())), preferred_element_type=F32
            ).astype(BF16)
        store = pltpu.make_async_copy(target, home, osem.at[c])
        store.start()
        stores.append(store)

    steps = dict(
        first=first, weights=weights, relay=relay, up=up, rowsum=rowsum, act=act_step, spread=spread,
        down=down, pair=pair, colsum=colsum, finish=finish, grad=grad,
    )
    steps["pass"] = pass_on
    for name, c, d in ORDER:
        steps[name](c, d)
    for store in stores:
        store.wait()
    for copy in sends:
        copy.wait_send()


def shards(inputs, up_weight, down_weight, out_grad):
    t, dm = inputs.shape
    ff = up_weight.shape[1]
    vmem = pl.BlockSpec(memory_space=pltpu.VMEM)
    anywhere = pl.BlockSpec(memory_space=pl.ANY)
    dma = pltpu.SemaphoreType.DMA
    outputs, in_grad, up_grad, down_grad = pl.pallas_call(
        kernel,
        out_shape=(
            jax.ShapeDtypeStruct((t, dm), BF16),
            jax.ShapeDtypeStruct((t, dm), BF16),
            jax.ShapeDtypeStruct((dm, ff), BF16),
            jax.ShapeDtypeStruct((ff, dm), BF16),
        ),
        in_specs=[vmem, vmem, anywhere, anywhere],
        out_specs=(vmem, vmem, anywhere, anywhere),
        scratch_shapes=[
            pltpu.VMEM((dm, ff), BF16),
            pltpu.VMEM((ff, dm), BF16),
            pltpu.VMEM((ff, dm), BF16),
            pltpu.VMEM((dm, ff), BF16),
            pltpu.VMEM((2, 4, 128, dm), BF16),
            pltpu.VMEM((2, 4, 128, ff), F32),
            pltpu.VMEM((2, 4, 128, ff), BF16),
            pltpu.VMEM((2, 4, 3, 32, ff), BF16),
            pltpu.VMEM((2, 4, 32, ff), F32),
            pltpu.VMEM((2, 4, 16, ff), BF16),
            pltpu.VMEM((2, 4, 16, ff), BF16),
            pltpu.VMEM((4, 16, ff), F32),
            pltpu.VMEM((2, 4, 128, ff), BF16),
            pltpu.VMEM((2, 4, 128, dm), F32),
            pltpu.VMEM((2, 4, 64, dm), F32),
            pltpu.VMEM((2, 3, 64, dm), BF16),
            pltpu.VMEM((2, 3, 64, dm), BF16),
            pltpu.VMEM((2, 64, dm), F32),
            pltpu.VMEM((2, 64, dm), BF16),
            pltpu.VMEM((2, 3, 16, dm), BF16),
            pltpu.VMEM((8, 128), F32),
            pltpu.VMEM((dm, ff), BF16),
            pltpu.VMEM((ff, dm), BF16),
            dma((2,)),
            dma((2,)),
            dma((160,)),
            dma((2, 3)),
            dma((2, 4, 4)),
            dma((2, 4)),
            dma((2, 4)),
            dma((2, 4, 3)),
            dma((2, 4)),
            dma((2, 4)),
            dma((2, 4, 3)),
            dma((2, 4)),
            dma((2, 3)),
            dma((2, 3)),
        ],
        compiler_params=pltpu.CompilerParams(
            collective_id=0, has_side_effects=True, vmem_limit_bytes=58 << 20
        ),
        name="block",
    )(inputs, out_grad, up_weight, down_weight)
    return outputs, in_grad, up_grad, down_grad


def solution(mesh):
    in_specs = (P("col", "row"), P("row", "col"), P("col", "row"), P("col", "row"))
    out_specs = (P("col", "row"), P("col", "row"), P("row", "col"), P("col", "row"))
    return jax.shard_map(shards, mesh=mesh, in_specs=in_specs, out_specs=out_specs, check_vma=False)
```

time: 613 us -> 99.9 us (0.16)
  the two profiles are of different devices: /device:TPU:1 before, /device:TPU:31 now
where the time goes in v1:
time: 99.9 us; the launch traced here: 99.6 us
  Pallas kernels  91.3 us (91%)
  local copies, waits for them, and re-layouts  7.62 us (8%)
    pallas_call x1, Pallas kernels, shards(): pl.pallas_call(kernel, out_shape=(jax.ShapeDtypeStruct((t, dm), BF16), ja...  91.3 us
    unnamed x6, local copies, waits for them, and re-layouts  7.62 us

profile of v1, /device:TPU:31, one launch (start us, length us, event | category | flops | bytes accessed | tf_op | source)
XLA Modules:
  0.0 99.6 jit_solution(7272664526496472690)
XLA Ops:
  0.6 91.3 %block.1 = (bf16[16,1536]{1,0:T(8,128)(2,1)}, bf16[16,1536]{1,0:T(8,128)(2,1)}, bf16[1536,768]{1,0:T(8,128)(2,1)}, bf16[768,1536]{1,0:T(8,128)(2,1)}) custom-call(bf16[16,1536]{1,0:T(8,128)(2,1)} %x_ref.1, bf16[16,1536]{1,0:T(8,128)(2,1)} %g_ref.1, bf16[1536,768]{1,0:T(8,128)(2,1)} %wu_hbm.1, bf16[768,1536]{1,0:T(8,128)(2,1)} %wd_hbm.1), custom_call_target="tpu_custom_call" | custom-call | tf_op jit(solution)/shard_map/block/pallas_call | solution.py:238
  92.0 1.4 %copy.12 = bf16[16,1536]{1,0:T(8,128)(2,1)} copy(bf16[16,1536]{1,0:T(8,128)(2,1)} %get-tuple-element.8) | data formatting | bytes 98304
  93.4 1.4 %copy.13 = bf16[16,1536]{1,0:T(8,128)(2,1)} copy(bf16[16,1536]{1,0:T(8,128)(2,1)} %get-tuple-element.9) | data formatting | bytes 98304
  94.8 0.0 copy-start
  94.8 3.4 %copy.14 = bf16[1536,768]{1,0:T(8,128)(2,1)} copy(bf16[1536,768]{1,0:T(8,128)(2,1)} %get-tuple-element.10) | data formatting | bytes 4718592
  98.2 0.0 copy-done
  98.2 1.4 %copy.15 = bf16[768,1536]{1,0:T(8,128)(2,1)} copy(bf16[768,1536]{1,0:T(8,128)(2,1)S(1)} %copy-done) | data formatting | bytes 4718592
Async XLA Ops:
  94.8 3.4 %copy-start = (bf16[768,1536]{1,0:T(8,128)(2,1)S(1)}, bf16[768,1536]{1,0:T(8,128)(2,1)}, u32[]{:S(2)}) copy-start(bf16[768,1536]{1,0:T(8,128)(2,1)} %get-tuple-element.11) | copy-start | bytes 7077892

commit v2 on v1

v2 whole, which is shorter than its diff:
```python
import functools

import jax
import jax.numpy as jnp
from jax import lax
from jax.experimental import pallas as pl
from jax.experimental.pallas import tpu as pltpu
from jax.sharding import PartitionSpec as P

MESH = pl.DeviceIdType.MESH
F32, BF16 = jnp.float32, jnp.bfloat16

gelu_coef = 0.7978845608
cube_coef = 0.044715

ORDER = (
    ("first", 0, 0), ("first", 1, 0), ("weights", 0, 0), ("relay", 0, 1), ("relay", 0, 2), ("relay", 0, 3),
    ("relay", 1, 1), ("up", 0, 0), ("pass", 0, 1), ("pass", 0, 3), ("relay", 1, 2), ("relay", 1, 3), ("up", 0, 1),
    ("up", 0, 3), ("rowsum", 0, 0), ("pass", 0, 2), ("up", 0, 2), ("pass", 1, 1), ("pass", 1, 3), ("rowsum", 0, 1),
    ("up", 1, 1), ("rowsum", 0, 3), ("up", 1, 3), ("pass", 1, 2), ("rowsum", 0, 2), ("up", 1, 2), ("act", 0, 1),
    ("rowsum", 1, 1), ("act", 0, 3), ("rowsum", 1, 3), ("up", 1, 0), ("act", 0, 2), ("rowsum", 1, 2), ("down", 0, 1),
    ("act", 1, 1), ("down", 0, 3), ("pair", 0, 1), ("act", 1, 2), ("rowsum", 1, 0), ("act", 0, 0), ("act", 1, 3),
    ("pair", 0, 3), ("down", 0, 2), ("pair", 0, 2), ("down", 1, 1), ("act", 1, 0), ("down", 1, 2), ("pair", 1, 2),
    ("down", 0, 0), ("grad", 0, 0), ("down", 1, 3), ("pair", 1, 1), ("pair", 0, 0), ("colsum", 0, 0),
    ("colsum", 0, 1), ("colsum", 0, 3), ("colsum", 0, 2), ("pair", 1, 3), ("down", 1, 0), ("grad", 1, 0),
    ("pair", 1, 0), ("colsum", 1, 0), ("colsum", 1, 1), ("finish", 0, 0), ("colsum", 1, 2), ("colsum", 1, 3),
    ("finish", 1, 0),
)


def kernel(
    x_ref, g_ref, wu_hbm, wd_hbm,
    out_ref, in_grad_ref, up_grad, down_grad,
    wu, wd, wut, wdt, gather, part, send_x, recv_x, own_x, send_z, recv_z, slopes, act,
    prod, recv_c, send_y, recv_y, own_y, send_f, recv_f, own_f,
    wsem, sent, gz, gy, gf, gs, gs0, rx, rz, ax, rc, ry, rf,
):
    row, col = lax.axis_index("row"), lax.axis_index("col")
    x, h = lax.rem(row, 4), row // 4
    y, zl, k = col // 8, lax.rem(col // 2, 4), lax.rem(col, 2)

    def at(dx=0, dh=0, dy=0, dz=0, dk=0):
        r = lax.rem(h + dh, 2) * 4 + lax.rem(x + dx, 4)
        c = lax.rem(y + dy, 4) * 8 + lax.rem(zl + dz, 4) * 2 + lax.rem(k + dk, 2)
        return (r, c)

    loads = [
        pltpu.make_async_copy(wu_hbm, wu, wsem.at[0]),
        pltpu.make_async_copy(wd_hbm, wd, wsem.at[1]),
    ]
    for load in loads:
        load.start()

    barrier = pltpu.get_barrier_semaphore()
    partners = [dict(dk=1), dict(dh=1)]
    for j in (1, 2, 3):
        partners += [dict(dx=j), dict(dy=j), dict(dz=j)]
    for partner in partners:
        pl.semaphore_signal(barrier, inc=1, device_id=at(**partner), device_id_type=MESH)
    pl.semaphore_wait(barrier, len(partners))

    sends = []

    def send(src, dst, sem, **where):
        copy = pltpu.make_async_remote_copy(
            src_ref=src, dst_ref=dst, send_sem=sent.at[len(sends)], recv_sem=sem,
            device_id=at(**where), device_id_type=MESH,
        )
        copy.start()
        sends.append(copy)

    def arrive(dst, sem):
        pltpu.make_async_remote_copy(
            src_ref=dst, dst_ref=dst, send_sem=sent.at[0], recv_sem=sem,
            device_id=at(dk=1), device_id_type=MESH,
        ).wait_recv()

    def rows(start, size):
        return pl.ds(pl.multiple_of(start, 16), size)

    def place(core, z):
        return rows(core * 64 + z * 16, 16)

    sources = (x_ref, g_ref)

    def first(c, _):
        src = sources[c]
        for j in (1, 2, 3):
            send(src, gather.at[c, 0, place(k, zl)], gz.at[c, j - 1], dz=j)
        for d in (1, 3):
            send(src, gather.at[c, 4 - d, place(k, zl)], gy.at[c, 4 - d, 0], dy=d)
        send(src, gather.at[c, 0, place(k, zl)], gs0.at[c, 0], dk=1)
        gather[c, 0, place(k, zl)] = src[...]

    def weights(c, _):
        for load in loads:
            load.wait()
        for j in range(3):
            wut[j * 256:(j + 1) * 256, :] = wu[:, j * 256:(j + 1) * 256].T
        for j in range(6):
            wdt[j * 256:(j + 1) * 256, :] = wd[:, j * 256:(j + 1) * 256].T

    def relay(c, j):
        piece = gather.at[c, 0, place(k, lax.rem(zl + 4 - j, 4))]
        arrive(piece, gz.at[c, j - 1])
        for d in (1, 3):
            send(piece, gather.at[c, 4 - d, place(k, lax.rem(zl + 4 - j, 4))], gy.at[c, 4 - d, j], dy=d)
        send(piece, piece, gs0.at[c, j], dk=1)

    def pass_on(c, d):
        if d == 2:
            for side in (0, 1):
                arrive(gather.at[c, 2, rows(k * 64 + side * 32, 32)], gf.at[c, side])
        else:
            for j in range(4):
                arrive(gather.at[c, d, place(k, lax.rem(zl + 4 - j, 4))], gy.at[c, d, j])
            side = 0 if d == 3 else 1
            piece = rows(k * 64 + side * 32, 32)
            send(gather.at[c, d, piece], gather.at[c, 2, piece], gf.at[c, side], dy=4 - d)
        half = gather.at[c, d, rows(k * 64, 64)]
        send(half, half, gs.at[c, d], dk=1)

    def up(c, d):
        if d == 0:
            for j in range(4):
                arrive(gather.at[c, 0, place(1 - k, lax.rem(zl + 4 - j, 4))], gs0.at[c, j])
        else:
            arrive(gather.at[c, d, rows((1 - k) * 64, 64)], gs.at[c, d])
        weight = (wu, wdt)[c]
        part[c, d] = jnp.dot(gather[c, d], weight[...], preferred_element_type=F32)
        send_x[c, d] = part[c, d].astype(BF16)
        for j in (1, 3, 2):
            send(send_x.at[c, d, rows(lax.rem(x + j, 4) * 32, 32)], recv_x.at[c, d, j - 1], rx.at[c, d, j - 1], dx=j)

    def rowsum(c, d):
        for j in (1, 2, 3):
            arrive(recv_x.at[c, d, j - 1], rx.at[c, d, j - 1])
        total = part[c, d, rows(x * 32, 32)]
        for j in (1, 2, 3):
            total = total + recv_x[c, d, j - 1].astype(F32)
        own_x[c, d] = total
        send_z[c, d] = total.astype(BF16)
        send(send_z.at[c, d], recv_z.at[c, d], rz.at[c, d], dh=1)

    def act_step(c, d):
        arrive(recv_z.at[c, d], rz.at[c, d])
        total = own_x[c, d] + recv_z[c, d].astype(F32)
        if c == 0:
            tangent = jnp.tanh(gelu_coef * (total + cube_coef * total * total * total))
            inner = gelu_coef * (1.0 + 3.0 * cube_coef * total * total)
            slopes[d] = 0.5 * (1.0 + tangent) + 0.5 * total * (1.0 - tangent * tangent) * inner
            result = 0.5 * total * (1.0 + tangent)
        else:
            result = total * slopes[d]
        mine = rows(x * 32, 32)
        act[c, d, mine] = result.astype(BF16)
        for j in (1, 3, 2):
            send(act.at[c, d, mine], act.at[c, d, mine], ax.at[c, d, j - 1], dx=j)

    def down(c, d):
        for j in (1, 2, 3):
            arrive(act.at[c, d, rows(lax.rem(x + 4 - j, 4) * 32, 32)], ax.at[c, d, j - 1])
        weight = (wd, wut)[c]
        prod[c, d] = jnp.dot(act[c, d], weight[...], preferred_element_type=F32)
        send(prod.at[c, d, rows((1 - k) * 64, 64)], recv_c.at[c, d], rc.at[c, d], dk=1)

    def pair(c, d):
        arrive(recv_c.at[c, d], rc.at[c, d])
        total = prod[c, d, rows(k * 64, 64)] + recv_c[c, d]
        if d == 0:
            own_y[c] = total
        else:
            send_y[c, d - 1] = total.astype(BF16)
            for j in (1, 2, 3, 0):
                piece = rows(lax.rem(zl + j, 4) * 16, 16)
                send(send_y.at[c, d - 1, piece], recv_y.at[c, d - 1, piece], ry.at[c, d - 1, j], dy=d)

    def colsum(c, p):
        j = (p + 1) % 4
        piece = rows(lax.rem(zl + j, 4) * 16, 16)
        for d in (1, 2, 3):
            arrive(recv_y.at[c, d - 1, piece], ry.at[c, d - 1, j])
        total = own_y[c, piece]
        for d in (1, 2, 3):
            total = total + recv_y[c, d - 1, piece].astype(F32)
        if j == 0:
            own_f[c] = total
        else:
            send_f[c, piece] = total.astype(BF16)
            send(send_f.at[c, piece], recv_f.at[c, j - 1], rf.at[c, j - 1], dz=j)

    results = (out_ref, in_grad_ref)

    def finish(c, _):
        for j in (1, 2, 3):
            arrive(recv_f.at[c, j - 1], rf.at[c, j - 1])
        total = own_f[c]
        for j in (1, 2, 3):
            total = total + recv_f[c, j - 1].astype(F32)
        results[c][...] = total.astype(BF16)

    def grad(c, _):
        left, right = ((act, gather), (gather, act))[c]
        target = (down_grad, up_grad)[c]
        a = left[0, :].reshape(512, left.shape[3])
        width = right.shape[3]
        for n in range(0, width, 256):
            b = right[1, :, :, n:n + 256].reshape(512, 256)
            target[:, n:n + 256] = lax.dot_general(
                a, b, (((0,), (0,)), ((), ())), preferred_element_type=F32
            ).astype(BF16)

    steps = dict(
        first=first, weights=weights, relay=relay, up=up, rowsum=rowsum, act=act_step,
        down=down, pair=pair, colsum=colsum, finish=finish, grad=grad,
    )
    steps["pass"] = pass_on
    for name, c, d in ORDER:
        steps[name](c, d)
    for copy in sends:
        copy.wait_send()


def store(*refs):
    sems = refs[8]
    copies = [pltpu.make_async_copy(refs[i], refs[4 + i], sems.at[i]) for i in range(4)]
    for copy in copies:
        copy.start()
    for copy in copies:
        copy.wait()


def shards(inputs, up_weight, down_weight, out_grad):
    t, dm = inputs.shape
    ff = up_weight.shape[1]
    vmem = pl.BlockSpec(memory_space=pltpu.VMEM)
    anywhere = pl.BlockSpec(memory_space=pl.ANY)
    dma = pltpu.SemaphoreType.DMA
    results = pl.pallas_call(
        kernel,
        out_shape=(
            pltpu.VMEM((t, dm), BF16),
            pltpu.VMEM((t, dm), BF16),
            pltpu.VMEM((dm, ff), BF16),
            pltpu.VMEM((ff, dm), BF16),
        ),
        in_specs=[vmem, vmem, anywhere, anywhere],
        out_specs=(vmem,) * 4,
        scratch_shapes=[
            pltpu.VMEM((dm, ff), BF16),
            pltpu.VMEM((ff, dm), BF16),
            pltpu.VMEM((ff, dm), BF16),
            pltpu.VMEM((dm, ff), BF16),
            pltpu.VMEM((2, 4, 128, dm), BF16),
            pltpu.VMEM((2, 4, 128, ff), F32),
            pltpu.VMEM((2, 4, 128, ff), BF16),
            pltpu.VMEM((2, 4, 3, 32, ff), BF16),
            pltpu.VMEM((2, 4, 32, ff), F32),
            pltpu.VMEM((2, 4, 32, ff), BF16),
            pltpu.VMEM((2, 4, 32, ff), BF16),
            pltpu.VMEM((4, 32, ff), F32),
            pltpu.VMEM((2, 4, 128, ff), BF16),
            pltpu.VMEM((2, 4, 128, dm), F32),
            pltpu.VMEM((2, 4, 64, dm), F32),
            pltpu.VMEM((2, 3, 64, dm), BF16),
            pltpu.VMEM((2, 3, 64, dm), BF16),
            pltpu.VMEM((2, 64, dm), F32),
            pltpu.VMEM((2, 64, dm), BF16),
            pltpu.VMEM((2, 3, 16, dm), BF16),
            pltpu.VMEM((2, 16, dm), F32),
            dma((2,)),
            dma((160,)),
            dma((2, 3)),
            dma((2, 4, 4)),
            dma((2, 2)),
            dma((2, 4)),
            dma((2, 4)),
            dma((2, 4, 3)),
            dma((2, 4)),
            dma((2, 4, 3)),
            dma((2, 4)),
            dma((2, 3, 4)),
            dma((2, 3)),
        ],
        compiler_params=pltpu.CompilerParams(
            collective_id=0, has_side_effects=True, vmem_limit_bytes=58 << 20
        ),
        name="block",
    )(inputs, out_grad, up_weight, down_weight)
    return pl.pallas_call(
        store,
        out_shape=tuple(jax.ShapeDtypeStruct(r.shape, r.dtype) for r in results),
        in_specs=[vmem] * 4,
        out_specs=(anywhere,) * 4,
        scratch_shapes=[dma((4,))],
        compiler_params=pltpu.CompilerParams(vmem_limit_bytes=1 << 20),
        name="store",
    )(*results)


def solution(mesh):
    in_specs = (P("col", "row"), P("row", "col"), P("col", "row"), P("col", "row"))
    out_specs = (P("col", "row"), P("col", "row"), P("row", "col"), P("col", "row"))
    return jax.shard_map(shards, mesh=mesh, in_specs=in_specs, out_specs=out_specs, check_vma=False)
```

time: 99.9 us -> 74.8 us (0.75)
  the two profiles are of different devices: /device:TPU:31 before, /device:TPU:1 now
where the time goes in v2:
time: 74.8 us; the launch traced here: 74.7 us
  Pallas kernels  74 us (99%)
    pallas_call x1, Pallas kernels, shards(): pl.pallas_call(kernel, out_shape=(pltpu.VMEM((t, dm), BF16), pltpu.VMEM((...  71.8 us
    pallas_call x1, Pallas kernels, shards(): pl.pallas_call(store, out_shape=tuple((jax.ShapeDtypeStruct(r.shape, r.dt...  2.25 us

profile of v2, /device:TPU:1, one launch (start us, length us, event | category | flops | bytes accessed | tf_op | source)
XLA Modules:
  0.0 74.7 jit_solution(5744656193946683947)
XLA Ops:
  0.6 71.8 %block.1 = (bf16[16,1536]{1,0:T(8,128)(2,1)S(1)}, bf16[16,1536]{1,0:T(8,128)(2,1)S(1)}, bf16[1536,768]{1,0:T(8,128)(2,1)S(1)}, bf16[768,1536]{1,0:T(8,128)(2,1)S(1)}) custom-call(bf16[16,1536]{1,0:T(8,128)(2,1)} %x_ref.1, bf16[16,1536]{1,0:T(8,128)(2,1)} %g_ref.1, bf16[1536,768]{1,0:T(8,128)(2,1)} %wu_hbm.1, bf16[768,1536]{1,0:T(8,128)(2,1)} %wd_hbm.1), custom_call_target="tpu_custom_call" | custom-call | tf_op jit(solution)/shard_map/block/pallas_call | solution.py:239
  72.4 2.3 %store.1 = (bf16[16,1536]{1,0:T(8,128)(2,1)}, bf16[16,1536]{1,0:T(8,128)(2,1)}, bf16[1536,768]{1,0:T(8,128)(2,1)}, bf16[768,1536]{1,0:T(8,128)(2,1)}) custom-call(bf16[16,1536]{1,0:T(8,128)(2,1)S(1)} %get-tuple-element.8.refs_0_, bf16[16,1536]{1,0:T(8,128)(2,1)S(1)} %get-tuple-element.9.refs_1_, bf16[1536,768]{1,0:T(8,128)(2,1)S(1)} %get-tuple-element.10.refs_2_, ...), custom_call_target="tpu_custom_call" | custom-call | tf_op jit(solution)/shard_map/store/pallas_call | solution.py:290

commit v3 on v2

--- a/solution.py
+++ b/solution.py
@@ -14,8 +14,8 @@
 cube_coef = 0.044715
 
 ORDER = (
-    ("first", 0, 0), ("first", 1, 0), ("weights", 0, 0), ("relay", 0, 1), ("relay", 0, 2), ("relay", 0, 3),
-    ("relay", 1, 1), ("up", 0, 0), ("pass", 0, 1), ("pass", 0, 3), ("relay", 1, 2), ("relay", 1, 3), ("up", 0, 1),
+    ("first", 0, 0), ("weights", 0, 0), ("relay", 0, 1), ("relay", 0, 2), ("relay", 0, 3), ("first", 1, 0),
+    ("up", 0, 0), ("pass", 0, 1), ("pass", 0, 3), ("relay", 1, 1), ("relay", 1, 2), ("relay", 1, 3), ("up", 0, 1),
     ("up", 0, 3), ("rowsum", 0, 0), ("pass", 0, 2), ("up", 0, 2), ("pass", 1, 1), ("pass", 1, 3), ("rowsum", 0, 1),
     ("up", 1, 1), ("rowsum", 0, 3), ("up", 1, 3), ("pass", 1, 2), ("rowsum", 0, 2), ("up", 1, 2), ("act", 0, 1),
     ("rowsum", 1, 1), ("act", 0, 3), ("rowsum", 1, 3), ("up", 1, 0), ("act", 0, 2), ("rowsum", 1, 2), ("down", 0, 1),
@@ -129,7 +129,7 @@
         weight = (wu, wdt)[c]
         part[c, d] = jnp.dot(gather[c, d], weight[...], preferred_element_type=F32)
         send_x[c, d] = part[c, d].astype(BF16)
-        for j in (1, 3, 2):
+        for j in (2, 1, 3):
             send(send_x.at[c, d, rows(lax.rem(x + j, 4) * 32, 32)], recv_x.at[c, d, j - 1], rx.at[c, d, j - 1], dx=j)
 
     def rowsum(c, d):
@@ -154,7 +154,7 @@
             result = total * slopes[d]
         mine = rows(x * 32, 32)
         act[c, d, mine] = result.astype(BF16)
-        for j in (1, 3, 2):
+        for j in (2, 1, 3):
             send(act.at[c, d, mine], act.at[c, d, mine], ax.at[c, d, j - 1], dx=j)
 
     def down(c, d):

time: 74.8 us -> 73.7 us (0.985)
  Pallas kernels: 74 us -> 72.9 us
    pallas_call x1, Pallas kernels: 71.8 us -> 70.6 us  [shards(): pl.pallas_call(kernel, out_shape=(pltpu.VMEM((t, dm), BF16), pltpu.VMEM((...]
where the time goes in v3:
time: 73.7 us; the launch traced here: 73.5 us
  Pallas kernels  72.9 us (99%)
    pallas_call x1, Pallas kernels, shards(): pl.pallas_call(kernel, out_shape=(pltpu.VMEM((t, dm), BF16), pltpu.VMEM((...  70.6 us
    pallas_call x1, Pallas kernels, shards(): pl.pallas_call(store, out_shape=tuple((jax.ShapeDtypeStruct(r.shape, r.dt...  2.25 us

profile of v3, /device:TPU:1, one launch (start us, length us, event | category | flops | bytes accessed | tf_op | source)
XLA Modules:
  0.0 73.5 jit_solution(419688798858314697)
XLA Ops:
  0.6 70.6 %block.1 = (bf16[16,1536]{1,0:T(8,128)(2,1)S(1)}, bf16[16,1536]{1,0:T(8,128)(2,1)S(1)}, bf16[1536,768]{1,0:T(8,128)(2,1)S(1)}, bf16[768,1536]{1,0:T(8,128)(2,1)S(1)}) custom-call(bf16[16,1536]{1,0:T(8,128)(2,1)} %x_ref.1, bf16[16,1536]{1,0:T(8,128)(2,1)} %g_ref.1, bf16[1536,768]{1,0:T(8,128)(2,1)} %wu_hbm.1, bf16[768,1536]{1,0:T(8,128)(2,1)} %wd_hbm.1), custom_call_target="tpu_custom_call" | custom-call | tf_op jit(solution)/shard_map/block/pallas_call | solution.py:239
  71.3 2.3 %store.1 = (bf16[16,1536]{1,0:T(8,128)(2,1)}, bf16[16,1536]{1,0:T(8,128)(2,1)}, bf16[1536,768]{1,0:T(8,128)(2,1)}, bf16[768,1536]{1,0:T(8,128)(2,1)}) custom-call(bf16[16,1536]{1,0:T(8,128)(2,1)S(1)} %get-tuple-element.8.refs_0_, bf16[16,1536]{1,0:T(8,128)(2,1)S(1)} %get-tuple-element.9.refs_1_, bf16[1536,768]{1,0:T(8,128)(2,1)S(1)} %get-tuple-element.10.refs_2_, ...), custom_call_target="tpu_custom_call" | custom-call | tf_op jit(solution)/shard_map/store/pallas_call | solution.py:290

commit v4 on v3

--- a/solution.py
+++ b/solution.py
@@ -19,7 +19,7 @@
     ("up", 0, 3), ("rowsum", 0, 0), ("pass", 0, 2), ("up", 0, 2), ("pass", 1, 1), ("pass", 1, 3), ("rowsum", 0, 1),
     ("up", 1, 1), ("rowsum", 0, 3), ("up", 1, 3), ("pass", 1, 2), ("rowsum", 0, 2), ("up", 1, 2), ("act", 0, 1),
     ("rowsum", 1, 1), ("act", 0, 3), ("rowsum", 1, 3), ("up", 1, 0), ("act", 0, 2), ("rowsum", 1, 2), ("down", 0, 1),
-    ("act", 1, 1), ("down", 0, 3), ("pair", 0, 1), ("act", 1, 2), ("rowsum", 1, 0), ("act", 0, 0), ("act", 1, 3),
+    ("act", 1, 1), ("down", 0, 3), ("pair", 0, 1), ("act", 1, 2), ("rowsum", 1, 0), ("act", 1, 3), ("act", 0, 0),
     ("pair", 0, 3), ("down", 0, 2), ("pair", 0, 2), ("down", 1, 1), ("act", 1, 0), ("down", 1, 2), ("pair", 1, 2),
     ("down", 0, 0), ("grad", 0, 0), ("down", 1, 3), ("pair", 1, 1), ("pair", 0, 0), ("colsum", 0, 0),
     ("colsum", 0, 1), ("colsum", 0, 3), ("colsum", 0, 2), ("pair", 1, 3), ("down", 1, 0), ("grad", 1, 0),

time: 73.7 us -> 74.7 us (1.014)
  Pallas kernels: 72.9 us -> 73.9 us
    pallas_call x1, Pallas kernels: 70.6 us -> 71.6 us  [shards(): pl.pallas_call(kernel, out_shape=(pltpu.VMEM((t, dm), BF16), pltpu.VMEM((...]
where the time goes in v4:
time: 74.7 us; the launch traced here: 74.5 us
  Pallas kernels  73.9 us (99%)
    pallas_call x1, Pallas kernels, shards(): pl.pallas_call(kernel, out_shape=(pltpu.VMEM((t, dm), BF16), pltpu.VMEM((...  71.6 us
    pallas_call x1, Pallas kernels, shards(): pl.pallas_call(store, out_shape=tuple((jax.ShapeDtypeStruct(r.shape, r.dt...  2.25 us

profile of v4, /device:TPU:1, one launch (start us, length us, event | category | flops | bytes accessed | tf_op | source)
XLA Modules:
  0.0 74.5 jit_solution(15503483055206446622)
XLA Ops:
  0.6 71.6 %block.1 = (bf16[16,1536]{1,0:T(8,128)(2,1)S(1)}, bf16[16,1536]{1,0:T(8,128)(2,1)S(1)}, bf16[1536,768]{1,0:T(8,128)(2,1)S(1)}, bf16[768,1536]{1,0:T(8,128)(2,1)S(1)}) custom-call(bf16[16,1536]{1,0:T(8,128)(2,1)} %x_ref.1, bf16[16,1536]{1,0:T(8,128)(2,1)} %g_ref.1, bf16[1536,768]{1,0:T(8,128)(2,1)} %wu_hbm.1, bf16[768,1536]{1,0:T(8,128)(2,1)} %wd_hbm.1), custom_call_target="tpu_custom_call" | custom-call | tf_op jit(solution)/shard_map/block/pallas_call | solution.py:239
  72.3 2.3 %store.1 = (bf16[16,1536]{1,0:T(8,128)(2,1)}, bf16[16,1536]{1,0:T(8,128)(2,1)}, bf16[1536,768]{1,0:T(8,128)(2,1)}, bf16[768,1536]{1,0:T(8,128)(2,1)}) custom-call(bf16[16,1536]{1,0:T(8,128)(2,1)S(1)} %get-tuple-element.8.refs_0_, bf16[16,1536]{1,0:T(8,128)(2,1)S(1)} %get-tuple-element.9.refs_1_, bf16[1536,768]{1,0:T(8,128)(2,1)S(1)} %get-tuple-element.10.refs_2_, ...), custom_call_target="tpu_custom_call" | custom-call | tf_op jit(solution)/shard_map/store/pallas_call | solution.py:290
